TPU v7x, 128 devices: a whole 4x4x4 slice. The times are simulated.
128 devices in a mesh: ctx: 32 (over x_lo, y, z), fsdp: 4 (over x_hi, core).
Axes of the slice: x: 4 (x_hi: 2, x_lo: 2; x = x_hi * 2 + x_lo), y: 4, z: 4, core: 2. Of those that a mesh axis runs over, the one named last changes fastest.
Arguments:
- tokens: bfloat16 [32, 4, 128, 1024], P('ctx', 'fsdp'), may hold values from -6 to 6
- block_order: int32 [32], replicated, may hold values from 0 to 31, each once
- weight_qkv: bfloat16 [1024, 3072], P('fsdp'), may hold values from -0.1875 to 0.1875
- bias_qkv: bfloat16 [3072], P('fsdp'), may hold values from -2 to 2
- weight_dense: bfloat16 [1024, 1024], P('fsdp'), may hold values from -3 to 3
- bias_dense: bfloat16 [1024], P('fsdp'), may hold values from -3 to 3
- weight_up: bfloat16 [1024, 4096], P('fsdp'), may hold values from -0.1875 to 0.1875
- bias_up: bfloat16 [4096], P('fsdp'), may hold values from -3 to 3
- weight_down: bfloat16 [1024, 4096], P('fsdp'), may hold values from -0.09375 to 0.09375
- bias_down: bfloat16 [1024], P('fsdp'), may hold values from -3 to 3
- gain_one: bfloat16 [1024], P('fsdp'), may hold values from 0.5 to 1.5
- shift_one: bfloat16 [1024], P('fsdp'), may hold values from -2 to 2
- gain_two: bfloat16 [1024], P('fsdp'), may hold values from 0.5 to 1.5
- shift_two: bfloat16 [1024], P('fsdp'), may hold values from -2 to 2
- cotangent: bfloat16 [32, 4, 128, 1024], P('ctx', 'fsdp'), may hold values from -6 to 6
Outputs:
- out_block: bfloat16 [32, 4, 128, 1024], P('ctx', 'fsdp')
- grad_tokens: bfloat16 [32, 4, 128, 1024], P('ctx', 'fsdp')
- grad_weight_qkv: float32 [1024, 3072], P('fsdp')
- grad_bias_qkv: float32 [3072], P('fsdp')
- grad_weight_dense: float32 [1024, 1024], P('fsdp')
- grad_bias_dense: float32 [1024], P('fsdp')
- grad_weight_up: float32 [1024, 4096], P('fsdp')
- grad_bias_up: float32 [4096], P('fsdp')
- grad_weight_down: float32 [1024, 4096], P('fsdp')
- grad_bias_down: float32 [1024], P('fsdp')
- grad_gain_one: float32 [1024], P('fsdp')
- grad_shift_one: float32 [1024], P('fsdp')
- grad_gain_two: float32 [1024], P('fsdp')
- grad_shift_two: float32 [1024], P('fsdp')
Inputs may be any that keep to these rules, and one draw needn't show every extreme that they name: block_order names each of 0 to 31 once.
All inputs are finite; a program needn't handle non-finite values.
Results may differ from a plain program's by a relative error of at most 0.025.
Values may be sent and summed in bfloat16 or wider, within the bound.
No kernel may reach another device: no remote copies, remote signals or barrier semaphores. Data moves between devices by JAX's collectives and lax.ppermute only.
A program may use at most 192 MiB of HBM per device.

v0:
```python
import jax
import jax.numpy as jnp
from jax import lax
from jax.sharding import PartitionSpec as P

HEADS = 16
HEAD_DIM = 64
ROT_DIMS = 16


EPSILON = 1e-05
NEGATIVE = -1e30


def layer_norm(inputs, scaling, offsets):
    centre = inputs - jnp.mean(inputs, axis=-1, keepdims=True)
    spread = jnp.mean(centre * centre, axis=-1, keepdims=True)
    return centre * lax.rsqrt(spread + EPSILON) * scaling + offsets


def rotary(inputs, cosines, sine_vals):
    halfway = cosines.shape[-1] // 2
    turned = inputs[..., : 2 * halfway]
    swapped = jnp.concatenate([-turned[..., halfway:], turned[..., :halfway]], axis=-1)
    turned = turned * cosines + swapped * sine_vals
    return jnp.concatenate([turned, inputs[..., 2 * halfway :]], axis=-1)


def angles(places):
    halfway = ROT_DIMS // 2
    inverse = 10000.0 ** (-2.0 * jnp.arange(halfway).astype(places.dtype) / ROT_DIMS)
    phases = places[:, None] * inverse[None, :]
    phases = jnp.concatenate([phases, phases], axis=-1)
    return (jnp.cos(phases)[:, None, :], jnp.sin(phases)[:, None, :])


def score_grads(
    query_seg, grad_seg, total_seg, delta_seg, key_seg, value_seg, allowed, score_scale
):
    scores = (
        jnp.einsum("qhd,khd->qhk", query_seg, key_seg, preferred_element_type=jnp.float32)
        * score_scale
    )
    scores = jnp.where(allowed, scores, NEGATIVE)
    probability = jnp.where(allowed, jnp.exp(scores - total_seg), 0.0)
    grad_prob = jnp.einsum("qhd,khd->qhk", grad_seg, value_seg, preferred_element_type=jnp.float32)
    grad_score = (probability * (grad_prob - delta_seg)).astype(jnp.bfloat16)
    return (probability, grad_score)


def on_device(
    tokens,
    block_order,
    weight_qkv,
    bias_qkv,
    weight_dense,
    bias_dense,
    weight_up,
    bias_up,
    weight_down,
    bias_down,
    gain_one,
    shift_one,
    gain_two,
    shift_two,
    cotangent,
):
    rows_here = tokens.shape[2]
    model_width = tokens.shape[3]
    blocks = lax.axis_size("ctx")
    length = blocks * rows_here
    score_scale = HEAD_DIM ** (-0.5)
    inputs = tokens.reshape(rows_here, model_width).astype(jnp.float32)
    incoming = cotangent.reshape(rows_here, model_width)
    row_offsets = jnp.arange(rows_here, dtype=jnp.int32)
    key_places = (block_order[:, None] * rows_here + row_offsets[None, :]).reshape(length)
    my_places = lax.dynamic_slice_in_dim(key_places, lax.axis_index("ctx") * rows_here, rows_here)
    cosines, sine_vals = angles(my_places.astype(jnp.float32))
    gathered_params = (
        lax.all_gather(weight_qkv, "fsdp", axis=0, tiled=True),
        lax.all_gather(bias_qkv, "fsdp", axis=0, tiled=True),
        lax.all_gather(weight_dense, "fsdp", axis=0, tiled=True),
        lax.all_gather(bias_dense, "fsdp", axis=0, tiled=True),
        lax.all_gather(weight_up, "fsdp", axis=0, tiled=True),
        lax.all_gather(bias_up, "fsdp", axis=0, tiled=True),
        lax.all_gather(weight_down, "fsdp", axis=0, tiled=True),
        lax.all_gather(bias_down, "fsdp", axis=0, tiled=True),
        lax.all_gather(gain_one, "fsdp", axis=0, tiled=True),
        lax.all_gather(shift_one, "fsdp", axis=0, tiled=True),
        lax.all_gather(gain_two, "fsdp", axis=0, tiled=True),
        lax.all_gather(shift_two, "fsdp", axis=0, tiled=True),
    )
    (
        full_qkv,
        full_bqkv,
        full_dense,
        full_bdense,
        full_up,
        full_bup,
        full_down,
        full_bdown,
        full_gone,
        full_sone,
        full_gtwo,
        full_stwo,
    ) = gathered_params
    norm_one, norm_back_one = jax.vjp(
        layer_norm, inputs, full_gone.astype(jnp.float32), full_sone.astype(jnp.float32)
    )
    low_one = norm_one.astype(jnp.bfloat16)
    projected = jnp.dot(low_one, full_qkv, preferred_element_type=jnp.float32) + full_bqkv.astype(
        jnp.float32
    )
    projected = projected.reshape(rows_here, 3, HEADS, HEAD_DIM)
    queries = rotary(projected[:, 0], cosines, sine_vals).astype(jnp.bfloat16)
    key_rows = rotary(projected[:, 1], cosines, sine_vals).astype(jnp.bfloat16)
    values = projected[:, 2].astype(jnp.bfloat16)

    def absorb(current, segment):
        top_prev, total_prev, acc_prev = current
        key_seg, value_seg, place_seg = segment
        scores = (
            jnp.einsum("qhd,khd->qhk", queries, key_seg, preferred_element_type=jnp.float32)
            * score_scale
        )
        allowed = (place_seg[None, :] <= my_places[:, None])[:, None, :]
        scores = jnp.where(allowed, scores, NEGATIVE)
        top_new = jnp.maximum(top_prev, jnp.max(scores, axis=-1, keepdims=True))
        weights = jnp.where(allowed, jnp.exp(scores - top_new), 0.0)
        factor = jnp.exp(top_prev - top_new)
        total_new = total_prev * factor + jnp.sum(weights, axis=-1, keepdims=True)
        acc_new = acc_prev * factor + jnp.einsum(
            "qhk,khd->qhd",
            weights.astype(jnp.bfloat16),
            value_seg,
            preferred_element_type=jnp.float32,
        )
        return ((top_new, total_new, acc_new), None)

    start_state = (
        jnp.full((rows_here, HEADS, 1), NEGATIVE, jnp.float32),
        jnp.zeros((rows_here, HEADS, 1), jnp.float32),
        jnp.zeros((rows_here, HEADS, HEAD_DIM), jnp.float32),
    )
    running = start_state
    key_piece = lax.all_gather(key_rows.reshape(rows_here, model_width), "ctx", axis=0, tiled=True)
    value_piece = lax.all_gather(values.reshape(rows_here, model_width), "ctx", axis=0, tiled=True)
    row_count = key_piece.shape[0]
    attend_stride = min(512, row_count)
    number = row_count // attend_stride
    segments = (
        key_piece.reshape(number, attend_stride, HEADS, HEAD_DIM),
        value_piece.reshape(number, attend_stride, HEADS, HEAD_DIM),
        key_places.reshape(number, attend_stride),
    )
    running, ignored = lax.scan(absorb, running, segments)
    top_all, total_all, acc_all = running
    attended = acc_all / total_all
    log_total = top_all + jnp.log(total_all)
    att_low = attended.reshape(rows_here, model_width).astype(jnp.bfloat16)
    norm_two, norm_back_two = jax.vjp(
        layer_norm, inputs, full_gtwo.astype(jnp.float32), full_stwo.astype(jnp.float32)
    )
    low_two = norm_two.astype(jnp.bfloat16)
    upward = jnp.dot(low_two, full_up, preferred_element_type=jnp.float32) + full_bup.astype(
        jnp.float32
    )
    activated, gelu_back = jax.vjp(lambda pre_act: jax.nn.gelu(pre_act, approximate=False), upward)
    act_low = activated.astype(jnp.bfloat16)
    bias_total = full_bdense.astype(jnp.float32) + full_bdown.astype(jnp.float32)
    result = inputs + jnp.dot(att_low, full_dense, preferred_element_type=jnp.float32)
    result = (
        result
        + jnp.einsum("tf,df->td", act_low, full_down, preferred_element_type=jnp.float32)
        + bias_total
    )
    out_block = result.astype(jnp.bfloat16).reshape(tokens.shape)
    back_qkv, back_dense, back_up, back_down = (full_qkv, full_dense, full_up, full_down)
    grad_act = jnp.einsum("td,df->tf", incoming, back_down, preferred_element_type=jnp.float32)
    grad_up = gelu_back(grad_act)[0].astype(jnp.bfloat16)
    grad_att = jnp.einsum(
        "td,ed->te", incoming, back_dense, preferred_element_type=jnp.float32
    ).astype(jnp.bfloat16)
    grad_heads = grad_att.reshape(rows_here, HEADS, HEAD_DIM)
    row_delta = jnp.sum(grad_heads.astype(jnp.float32) * attended, axis=-1, keepdims=True)
    key_all, value_all = (
        lax.all_gather(key_rows.reshape(rows_here, model_width), "ctx", axis=0, tiled=True),
        lax.all_gather(values.reshape(rows_here, model_width), "ctx", axis=0, tiled=True),
    )
    stride = min(512, length)
    number = length // stride
    segments = (
        key_all.reshape(number, stride, HEADS, HEAD_DIM),
        value_all.reshape(number, stride, HEADS, HEAD_DIM),
        key_places.reshape(number, stride),
    )

    def back_step(grad_query, segment):
        key_seg, value_seg, place_seg = segment
        allowed = (place_seg[None, :] <= my_places[:, None])[:, None, :]
        probability, grad_score = score_grads(
            queries, grad_heads, log_total, row_delta, key_seg, value_seg, allowed, score_scale
        )
        grad_query = grad_query + jnp.einsum(
            "qhk,khd->qhd", grad_score, key_seg, preferred_element_type=jnp.float32
        )
        grad_key = (
            jnp.einsum("qhk,qhd->khd", grad_score, queries, preferred_element_type=jnp.float32)
            * score_scale
        )
        grad_value = jnp.einsum(
            "qhk,qhd->khd",
            probability.astype(jnp.bfloat16),
            grad_heads,
            preferred_element_type=jnp.float32,
        )
        return (
            grad_query,
            (grad_key.reshape(stride, model_width), grad_value.reshape(stride, model_width)),
        )

    grad_query, (grad_key_all, grad_value_all) = lax.scan(
        back_step, jnp.zeros((rows_here, HEADS, HEAD_DIM), jnp.float32), segments
    )
    grad_query = grad_query * score_scale
    grad_keys, grad_values = (
        lax.psum_scatter(
            grad_key_all.reshape(length, model_width).astype(jnp.bfloat16),
            "ctx",
            scatter_dimension=0,
            tiled=True,
        ).astype(jnp.float32),
        lax.psum_scatter(
            grad_value_all.reshape(length, model_width).astype(jnp.bfloat16),
            "ctx",
            scatter_dimension=0,
            tiled=True,
        ).astype(jnp.float32),
    )
    grad_query_raw = rotary(grad_query, cosines, -sine_vals)
    grad_key_raw = rotary(grad_keys.reshape(rows_here, HEADS, HEAD_DIM), cosines, -sine_vals)
    grad_qkv = jnp.stack(
        [grad_query_raw, grad_key_raw, grad_values.reshape(rows_here, HEADS, HEAD_DIM)], axis=1
    )
    grad_qkv = grad_qkv.reshape(rows_here, 3 * model_width).astype(jnp.bfloat16)
    grad_norm_one = jnp.einsum("tc,dc->td", grad_qkv, back_qkv, preferred_element_type=jnp.float32)
    grad_norm_two = jnp.einsum("tf,df->td", grad_up, back_up, preferred_element_type=jnp.float32)
    grad_in_one, grad_gone, grad_sone = norm_back_one(grad_norm_one)
    grad_in_two, grad_gtwo, grad_stwo = norm_back_two(grad_norm_two)
    grad_tokens = (
        (incoming.astype(jnp.float32) + grad_in_one + grad_in_two)
        .astype(jnp.bfloat16)
        .reshape(tokens.shape)
    )
    ff_width = grad_up.shape[1]
    bias_grad_dense = jnp.sum(incoming.astype(jnp.float32), axis=0)
    vector_parts = jnp.concatenate(
        [
            jnp.sum(grad_qkv.astype(jnp.float32), axis=0),
            bias_grad_dense,
            jnp.sum(grad_up.astype(jnp.float32), axis=0),
            grad_gone,
            grad_sone,
            grad_gtwo,
            grad_stwo,
        ]
    )
    vector_total = lax.psum(vector_parts, ("ctx", "fsdp"))
    shard_idx = lax.axis_index("fsdp")
    fsdp_count = lax.axis_size("fsdp")

    def own_part(offset_at, full_size):
        piece_size = full_size // fsdp_count
        return lax.dynamic_slice_in_dim(
            vector_total, offset_at + shard_idx * piece_size, piece_size
        )

    own_bqkv = own_part(0, 3 * model_width)
    own_bdense = own_part(3 * model_width, model_width)
    own_bup = own_part(4 * model_width, ff_width)
    own_gone = own_part(4 * model_width + ff_width, model_width)
    own_sone = own_part(5 * model_width + ff_width, model_width)
    own_gtwo = own_part(6 * model_width + ff_width, model_width)
    own_stwo = own_part(7 * model_width + ff_width, model_width)
    full_gqkv = jnp.einsum("td,tc->dc", low_one, grad_qkv, preferred_element_type=jnp.float32)
    full_gdense = jnp.einsum("td,te->de", att_low, incoming, preferred_element_type=jnp.float32)
    full_gup = jnp.einsum("td,tf->df", low_two, grad_up, preferred_element_type=jnp.float32)
    full_gdown = jnp.einsum("td,tf->df", incoming, act_low, preferred_element_type=jnp.float32)
    mat_qkv, mat_dense, mat_up, mat_down = (
        lax.psum_scatter(
            full_gqkv.astype(jnp.bfloat16), "fsdp", scatter_dimension=0, tiled=True
        ).astype(jnp.float32),
        lax.psum_scatter(
            full_gdense.astype(jnp.bfloat16), "fsdp", scatter_dimension=0, tiled=True
        ).astype(jnp.float32),
        lax.psum_scatter(
            full_gup.astype(jnp.bfloat16), "fsdp", scatter_dimension=0, tiled=True
        ).astype(jnp.float32),
        lax.psum_scatter(
            full_gdown.astype(jnp.bfloat16), "fsdp", scatter_dimension=0, tiled=True
        ).astype(jnp.float32),
    )
    mat_qkv, mat_dense, mat_up, mat_down = (
        lax.psum(mat_qkv.astype(jnp.bfloat16), "ctx").astype(jnp.float32),
        lax.psum(mat_dense.astype(jnp.bfloat16), "ctx").astype(jnp.float32),
        lax.psum(mat_up.astype(jnp.bfloat16), "ctx").astype(jnp.float32),
        lax.psum(mat_down.astype(jnp.bfloat16), "ctx").astype(jnp.float32),
    )
    return (
        out_block,
        grad_tokens,
        mat_qkv,
        own_bqkv,
        mat_dense,
        own_bdense,
        mat_up,
        own_bup,
        mat_down,
        own_bdense,
        own_gone,
        own_sone,
        own_gtwo,
        own_stwo,
    )


def solution(mesh):
    return jax.shard_map(
        on_device,
        mesh=mesh,
        in_specs=(
            P("ctx", "fsdp", None, None),
            P(),
            P("fsdp", None),
            P("fsdp"),
            P("fsdp", None),
            P("fsdp"),
            P("fsdp", None),
            P("fsdp"),
            P("fsdp", None),
            P("fsdp"),
            P("fsdp"),
            P("fsdp"),
            P("fsdp"),
            P("fsdp"),
            P("ctx", "fsdp", None, None),
        ),
        out_specs=(
            P("ctx", "fsdp", None, None),
            P("ctx", "fsdp", None, None),
            P("fsdp", None),
            P("fsdp"),
            P("fsdp", None),
            P("fsdp"),
            P("fsdp", None),
            P("fsdp"),
            P("fsdp", None),
            P("fsdp"),
            P("fsdp"),
            P("fsdp"),
            P("fsdp"),
            P("fsdp"),
        ),
        check_vma=False,
    )
```

profile of v0, /device:TPU:2, one launch (start us, length us, event | category | flops | bytes accessed | tf_op | source)
XLA Modules:
  0.0 1677.7 jit_solution(3124832242768998453)
XLA Ops:
  8.8 6.7 all-gather.2
  15.5 6.6 all-gather.1
  22.1 6.6 all-gather
  29.9 31.7 %all-gather.14.cloned.1.call-done = bf16[1024,3072]{1,0:T(8,128)(2,1)} async-done(((bf16[256,3072]{1,0:T(8,128)(2,1)}), bf16[1024,3072]{1,0:T(8,128)(2,1)}) %all-gather.14.cloned.1.call-update) | async-done | bytes 6291472 | tf_op jit(solution)/shard_map/all_gather | solution.py:80
  61.7 3.9 convolution_add_fusion.1
  69.5 19.9 %all-gather.20.cloned.1.call-done = bf16[1024,1024]{1,0:T(8,128)(2,1)} async-done(((bf16[256,1024]{1,0:T(8,128)(2,1)}), bf16[1024,1024]{1,0:T(8,128)(2,1)}) %all-gather.20.cloned.1.call-update) | async-done | bytes 2097168 | tf_op jit(solution)/shard_map/all_gather | solution.py:82
  92.7 168.1 %all-gather.16.cloned.1.call-done = bf16[4096,1024]{0,1:T(8,128)(2,1)} async-done(((bf16[128,1024]{0,1:T(8,128)(2,1)}), bf16[4096,1024]{0,1:T(8,128)(2,1)}) %all-gather.16.cloned.1.call-update) | async-done | bytes 8388624 | tf_op jit(solution)/shard_map/all_gather | solution.py:146
  260.9 12.2 copy.93
  273.0 9.6 copy.61
  282.6 152.0 %all-gather.18.cloned.1.call-done = bf16[4096,1024]{0,1:T(8,128)(2,1)} async-done(((bf16[128,1024]{0,1:T(8,128)(2,1)}), bf16[4096,1024]{0,1:T(8,128)(2,1)}) %all-gather.18.cloned.1.call-update) | async-done | bytes 8388624 | tf_op jit(solution)/shard_map/all_gather | solution.py:147
  434.7 12.4 copy.94
  447.1 10.7 copy.62
  457.7 86.1 %while.30 = (s32[]{:T(128)}, f32[128,16,1]{0,1,2:T(8,128)S(1)}, f32[128,16,1]{0,1,2:T(8,128)S(1)}, f32[128,16,64]{0,2,1:T(8,128)S(1)}, s32[8,512]{1,0:T(8,128)S(...) while((s32[]{:T(128)}, f32[128,16,1]{0,1,2:T(8,128)S(1)}, ...), condition=%wide.region_5.6_spmd.clone, body=%wide.region_2.5_spmd.clone.sunk | while | flops 282537984 | bytes 33168040 | solution.py:156
  458.3 4.2 fusion.173
  462.5 3.3 fusion.175
  468.8 4.2 fusion.173
  473.1 3.3 fusion.175
  479.4 4.2 fusion.173
  483.6 3.3 fusion.175
  489.9 4.2 fusion.173
  494.1 3.3 fusion.175
  500.4 4.2 fusion.173
  504.6 3.3 fusion.175
  510.9 4.3 fusion.173
  515.3 4.4 fusion.175
  522.8 4.2 fusion.173
  527.1 3.3 fusion.175
  533.5 4.2 fusion.173
  537.7 3.3 fusion.175
  545.6 149.4 %while.31 = (s32[]{:T(128)}, f32[128,16,64]{0,2,1:T(8,128)}, bf16[8,512,1024]{2,1,0:T(8,128)(2,1)}, bf16[8,512,1024]{2,1,0:T(8,128)(2,1)}, bf16[8,512,16,64]{1,3...) while((s32[]{:T(128)}, f32[128,16,64]{0,2,1:T(8,128)}, ...), condition=%wide.region_8.9_spmd.clone, body=%wide.region_7.8_spmd.clone.sunk | while | flops 685047808 | bytes 68385504 | solution.py:222
  547.8 4.1 fusion.188
  566.4 4.1 fusion.188
  585.1 4.1 fusion.188
  603.7 4.1 fusion.188
  622.5 4.1 fusion.188
  629.4 3.2 fusion.190
  641.1 4.1 fusion.188
  659.8 4.1 fusion.188
  666.8 3.2 fusion.190
  678.5 4.1 fusion.188
  685.4 3.2 fusion.190
  695.8 6.7 all_gather.54
  702.5 6.6 all-gather.4
  709.1 6.6 all-gather.3
  715.7 9.3 multiply_convert_fusion
  725.0 5.7 convert_bitcast_fusion
  730.8 8.7 convert_reduce_fusion
  739.5 5.8 convolution_convert_fusion
  749.7 127.4 %reduce-scatter.7.cloned.1.call-done = bf16[128,1024]{1,0:T(8,128)(2,1)} async-done(((bf16[4096,1024]{1,0:T(8,128)(2,1)}), bf16[128,1024]{1,0:T(8,128)(2,1)}) %reduce-scatter.7.cloned.1.call-update) | async-done | bytes 262160 | tf_op jit(solution)/shard_map/reduce_scatter | solution.py:227
  878.9 176.2 %reduce-scatter.9.cloned.1.call-done = bf16[128,1024]{1,0:T(8,128)(2,1)} async-done(((bf16[4096,1024]{1,0:T(8,128)(2,1)}), bf16[128,1024]{1,0:T(8,128)(2,1)}) %reduce-scatter.9.cloned.1.call-update) | async-done | bytes 262160 | tf_op jit(solution)/shard_map/reduce_scatter | solution.py:233
  1057.8 4.6 convolution_convert_fusion.1
  1062.4 70.6 %reduce-scatter.17.cloned.1.call-done = bf16[256,4096]{0,1:T(8,128)(2,1)} async-done(((bf16[1024,4096]{0,1:T(8,128)(2,1)}), bf16[256,4096]{0,1:T(8,128)(2,1)}) %reduce-scatter.17.cloned.1.call-update) | async-done | bytes 2097168 | tf_op jit(solution)/shard_map/reduce_scatter | solution.py:299
  1133.0 80.8 %reduce-scatter.15.cloned.1.call-done = bf16[256,4096]{1,0:T(8,128)(2,1)} async-done(((bf16[1024,4096]{1,0:T(8,128)(2,1)}), bf16[256,4096]{1,0:T(8,128)(2,1)}) %reduce-scatter.15.cloned.1.call-update) | async-done | bytes 2097168 | tf_op jit(solution)/shard_map/reduce_scatter | solution.py:296
  1213.9 41.0 %reduce-scatter.13.cloned.1.call-done = bf16[256,1024]{1,0:T(8,128)(2,1)} async-done(((bf16[1024,1024]{1,0:T(8,128)(2,1)}), bf16[256,1024]{1,0:T(8,128)(2,1)}) %reduce-scatter.13.cloned.1.call-update) | async-done | bytes 524304 | tf_op jit(solution)/shard_map/reduce_scatter | solution.py:293
  1254.9 67.4 %reduce-scatter.11.cloned.1.call-done = bf16[256,3072]{1,0:T(8,128)(2,1)} async-done(((bf16[1024,3072]{1,0:T(8,128)(2,1)}), bf16[256,3072]{1,0:T(8,128)(2,1)}) %reduce-scatter.11.cloned.1.call-update) | async-done | bytes 1572880 | tf_op jit(solution)/shard_map/reduce_scatter | solution.py:290
  1322.9 6.6 all-gather.6
  1329.5 6.6 all-gather.5
  1336.1 6.3 fusion.124
  1342.5 6.5 fusion.125
  1350.3 5.1 fusion.121
  1357.2 71.6 %psum.36 = f32[12288]{0:T(1024)S(1)} all-reduce(f32[12288]{0:T(1024)S(1)} %constant_dynamic-update-slice_fusion.2), channel_id=1, replica_groups=mesh['ctx'=32,'fsdp'=4] {'ctx','fsdp'}, use_global_device_ids=true, to_apply=%region_24.25 | all-reduce | flops 12288 | bytes 98304 | tf_op jit(solution)/shard_map/psum | solution.py:268
  1430.7 229.2 %all-reduce.3.cloned.1.call-done = (bf16[256,4096]{0,1:T(8,128)(2,1)}, bf16[256,3072]{1,0:T(8,128)(2,1)}, bf16[256,1024]{1,0:T(8,128)(2,1)}, bf16[256,4096]{1,0:T(8,128)(2,1)}) async-done(((bf16[256,4096]{0,1:T(8,128)(2,1)}, bf16[256,3072]{1,0:T(8,128)(2,1)}, bf16[256,1024]{1,0:T(8,128)(2,1)}, bf16[256,4096]{1,0:T(8,128)(2,1)}), (bf16[256,4096]{0,1:T(8,128)(2,1)}, bf16[256,3072]{1,0:T(8,128)(2,1)}, ...) | async-done | bytes 6291472 | tf_op jit(solution)/shard_map/psum | solution.py:307
  1659.9 3.6 convert_element_type.205
  1667.1 3.3 copy.70
  (333 shorter events, 161.4 us)
Async XLA Ops:
  7.2 1.6 copy-start.25
  7.2 8.3 copy-start.26
  7.2 14.9 copy-start.27
  7.2 21.5 %copy-start.28 = (s32[32]{0:T(128)S(1)}, s32[32]{0:T(128)}, u32[]{:S(2)}) copy-start(s32[32]{0:T(128)} %param.20) | copy-start | bytes 388
  7.2 22.4 %copy-start.3 = (bf16[1,1,128,1024]{3,2,1,0:T(8,128)(2,1)S(1)}, bf16[1,1,128,1024]{3,2,1,0:T(8,128)(2,1)}, u32[]{:S(2)}) copy-start(bf16[1,1,128,1024]{3,2,1,0:T(8,128)(2,1)} %param.19) | copy-start | bytes 786436
  7.2 54.4 %all-gather.14.cloned.1.call-start = ((), (), s32[]{:S(2)}) async-start(), calls=%async_computation.6 | async-start | bytes 7864320 | tf_op jit(solution)/shard_map/all_gather | solution.py:80
  8.0 81.4 %all-gather.20.cloned.1.call-start = ((), (), s32[]{:S(2)}) async-start(), calls=%async_computation.9 | async-start | bytes 2621440 | tf_op jit(solution)/shard_map/all_gather | solution.py:82
  8.7 252.1 %all-gather.16.cloned.1.call-start = ((), (), s32[]{:S(2)}) async-start(), calls=%async_computation.7 | async-start | bytes 8650752 | tf_op jit(solution)/shard_map/all_gather | solution.py:146
  22.1 39.6 %copy-start.16 = (f32[4,1,256]{2,1,0:T(1,128)}, f32[4,1,256]{2,1,0:T(1,128)S(1)}, u32[]{:S(2)}) copy-start(f32[4,1,256]{2,1,0:T(1,128)S(1)} %convert_element_type.216) | copy-start | bytes 12292
  28.7 33.0 %copy-start.13 = (f32[4,1,256]{2,1,0:T(1,128)}, f32[4,1,256]{2,1,0:T(1,128)S(1)}, u32[]{:S(2)}) copy-start(f32[4,1,256]{2,1,0:T(1,128)S(1)} %convert_element_type.215) | copy-start | bytes 12292
  29.6 36.6 %copy-start.18 = (f32[128,16]{0,1:T(8,128)}, f32[128,16]{0,1:T(8,128)S(1)}, u32[]{:S(2)}) copy-start(f32[128,16]{0,1:T(8,128)S(1)} %get-tuple-element.393) | copy-start | bytes 24580
  29.9 35.6 %copy-start.22 = (f32[128]{0:T(128)}, f32[128]{0:T(128)S(1)}, u32[]{:S(2)}) copy-start(f32[128]{0:T(128)S(1)} %fusion.79) | copy-start | bytes 1540
  67.0 367.7 %all-gather.18.cloned.1.call-start = ((), (), s32[]{:S(2)}) async-start(), calls=%async_computation.8 | async-start | bytes 8650752 | tf_op jit(solution)/shard_map/all_gather | solution.py:147
  67.8 21.6 %copy-start.8 = (bf16[1,1,128,1024]{3,2,1,0:T(8,128)(2,1)S(1)}, bf16[1,1,128,1024]{3,2,1,0:T(8,128)(2,1)}, u32[]{:S(2)}) copy-start(bf16[1,1,128,1024]{3,2,1,0:T(8,128)(2,1)} %param.33) | copy-start | bytes 786436
  67.9 647.8 %all-gather.22.cloned.1.call-start = ((), (), s32[]{:S(2)}) async-start(), calls=%async_computation.10 | async-start | bytes 10485760 | tf_op jit(solution)/shard_map/all_gather | solution.py:84
  68.4 662.4 %all-gather.24.cloned.1.call-start = ((), (), s32[]{:S(2)}) async-start(), calls=%async_computation.11 | async-start | bytes 10485760 | tf_op jit(solution)/shard_map/all_gather | solution.py:86
  69.0 808.1 %reduce-scatter.7.cloned.1.call-start = ((), (), s32[]{:S(2)}) async-start(), calls=%async_computation.12 | async-start | bytes 8650752 | tf_op jit(solution)/shard_map/reduce_scatter | solution.py:227
  462.5 3.5 copy-start
  473.0 3.5 copy-start
  483.6 3.5 copy-start
  494.1 3.5 copy-start
  504.6 3.5 copy-start
  515.3 4.7 copy-start
  527.0 3.5 copy-start
  537.7 3.5 copy-start
  547.6 4.3 copy-start.1
  551.9 2.7 copy-start.2
  566.2 4.3 copy-start.1
  570.5 2.9 copy-start.2
  584.9 4.3 copy-start.1
  589.2 2.9 copy-start.2
  603.6 4.3 copy-start.1
  607.9 2.9 copy-start.2
  622.3 4.3 copy-start.1
  626.6 2.9 copy-start.2
  641.0 4.3 copy-start.1
  645.3 2.9 copy-start.2
  659.6 4.3 copy-start.1
  663.9 2.9 copy-start.2
  678.3 4.3 copy-start.1
  682.6 2.9 copy-start.2
  695.0 360.1 %reduce-scatter.9.cloned.1.call-start = ((), (), s32[]{:S(2)}) async-start(), calls=%async_computation.13 | async-start | bytes 8650752 | tf_op jit(solution)/shard_map/reduce_scatter | solution.py:233
  695.1 7.4 copy-start.29
  695.1 14.0 copy-start.30
  695.1 20.6 %copy-start.4 = (bf16[1,1,128,1024]{3,2,1,0:T(8,128)(2,1)S(1)}, bf16[1,1,128,1024]{3,2,1,0:T(8,128)(2,1)}, u32[]{:S(2)}) copy-start(bf16[1,1,128,1024]{3,2,1,0:T(8,128)(2,1)} %param.19) | copy-start | bytes 786436
  695.8 437.2 %reduce-scatter.17.cloned.1.call-start = ((), (), s32[]{:S(2)}) async-start(), calls=%async_computation.17 | async-start | bytes 10485760 | tf_op jit(solution)/shard_map/reduce_scatter | solution.py:299
  715.7 9.3 copy-start.9
  730.7 483.1 %reduce-scatter.15.cloned.1.call-start = ((), (), s32[]{:S(2)}) async-start(), calls=%async_computation.16 | async-start | bytes 10485760 | tf_op jit(solution)/shard_map/reduce_scatter | solution.py:296
  739.5 5.8 copy-start.6
  745.3 1.0 copy-start.10
  745.3 509.5 %reduce-scatter.13.cloned.1.call-start = ((), (), s32[]{:S(2)}) async-start(), calls=%async_computation.15 | async-start | bytes 2621440 | tf_op jit(solution)/shard_map/reduce_scatter | solution.py:293
  748.3 308.0 %copy-start.19 = (f32[128,16]{0,1:T(8,128)S(1)}, f32[128,16]{0,1:T(8,128)}, u32[]{:S(2)}) copy-start(f32[128,16]{0,1:T(8,128)} %copy-done.18) | copy-start | bytes 24580
  748.3 308.0 %copy-start.20 = (f32[128,16]{0,1:T(8,128)S(1)}, f32[128,16]{0,1:T(8,128)}, u32[]{:S(2)}) copy-start(f32[128,16]{0,1:T(8,128)} %get-tuple-element.391) | copy-start | bytes 24580
  748.3 574.0 %reduce-scatter.11.cloned.1.call-start = ((), (), s32[]{:S(2)}) async-start(), calls=%async_computation.14 | async-start | bytes 7864320 | tf_op jit(solution)/shard_map/reduce_scatter | solution.py:290
  878.9 178.9 %copy-start.14 = (f32[4,1,256]{2,1,0:T(1,128)S(1)}, f32[4,1,256]{2,1,0:T(1,128)}, u32[]{:S(2)}) copy-start(f32[4,1,256]{2,1,0:T(1,128)} %copy-done.13) | copy-start | bytes 12292
  878.9 178.9 %copy-start.17 = (f32[4,1,256]{2,1,0:T(1,128)S(1)}, f32[4,1,256]{2,1,0:T(1,128)}, u32[]{:S(2)}) copy-start(f32[4,1,256]{2,1,0:T(1,128)} %copy-done.16) | copy-start | bytes 12292
  1062.4 597.5 %all-reduce.3.cloned.1.call-start = ((), (), s32[]{:S(2)}) async-start(), calls=%async_computation.18 | async-start | bytes 12582912 | tf_op jit(solution)/shard_map/psum | solution.py:307
  1336.1 6.4 copy-start.7
  1342.5 6.6 copy-start.5
  1350.3 5.1 copy-start.23
  1430.7 239.7 %copy-start.21 = (f32[256]{0:T(256)}, f32[256]{0:T(256)S(1)}, u32[]{:S(2)}) copy-start(f32[256]{0:T(256)S(1)} %get-tuple-element.639) | copy-start | bytes 3076
  1659.9 3.6 copy-start.15
  1659.9 4.7 copy-start.12
  1664.6 2.5 copy-start.11
  (3 other events, 2.1 us)
Sparse Core Ops, SparseCore 0:
  9.7 51.8 all-gather.13
  63.3 26.0 all-gather.19
  91.6 169.2 all-gather.15
  262.8 171.7 all-gather.17
  436.2 64.2 all-gather.21
  502.1 61.7 all-gather.23
  695.1 181.8 reduce-scatter.6
  879.5 175.5 reduce-scatter.8
  1057.8 75.1 reduce-scatter.16
  1135.8 78.0 reduce-scatter.14
  1217.1 37.7 reduce-scatter.12
  1257.5 64.6 reduce-scatter.10
  1325.0 334.7 all-reduce.2
where the time goes:
time: 1680 us
  waiting for transfers between devices  1170 us (70%)
  matrix products  228 us (14%)
  blocking collectives  124 us (7%)
  local copies, waits for them, and re-layouts  94.8 us (6%)
  other arithmetic  45.4 us (3%)
    psum x1, waiting for transfers between devices, on_device(): lax.psum(mat_down.astype(jnp.bfloat16), 'ctx').astype(jnp.float32)  229 us
    reduce_scatter x1, waiting for transfers between devices, on_device(): lax.psum_scatter(grad_value_all.reshape(length, model_width).astype(jnp.b...  176 us
    all_gather x1, waiting for transfers between devices, on_device(): lax.all_gather(key_rows.reshape(rows_here, model_width), 'ctx', axis=0, t...  168 us
    all_gather x1, waiting for transfers between devices, on_device(): lax.all_gather(values.reshape(rows_here, model_width), 'ctx', axis=0, til...  152 us
    reduce_scatter x1, waiting for transfers between devices, on_device(): lax.psum_scatter(grad_key_all.reshape(length, model_width).astype(jnp.bfl...  127 us
    reduce_scatter x1, waiting for transfers between devices, on_device(): lax.psum_scatter(full_gup.astype(jnp.bfloat16), 'fsdp', scatter_dimension...  80.8 us
    psum x1, blocking collectives, on_device(): vector_total = lax.psum(vector_parts, ('ctx', 'fsdp'))  71.6 us
    reduce_scatter x1, waiting for transfers between devices, on_device(): lax.psum_scatter(full_gdown.astype(jnp.bfloat16), 'fsdp', scatter_dimensi...  70.6 us
  transfers between devices with their start and end apart: 13, of which 11 were waited for; matrix products, arithmetic and copies ran while one was open for 21% of the time, Pallas kernels for 0%

commit v1 on v0

v1 whole, which is shorter than its diff:
```python
import jax
import jax.numpy as jnp
from jax import lax
from jax.experimental import pallas as pl
from jax.experimental.pallas import tpu as pltpu
from jax.sharding import PartitionSpec as P

HEADS = 16
HEAD_DIM = 64
ROT_DIMS = 16
EPSILON = 1e-05
NEGATIVE = -1e30
F32 = jnp.float32
BF16 = jnp.bfloat16

Q_TILE = 256
K_TILE = 512


def dot(a, b, ca=1, cb=0):
    return lax.dot_general(a, b, (((ca,), (cb,)), ((), ())), preferred_element_type=F32)


def attention_kernel(order_ref, recv_ref, out_ref, kv, kvt, qz, gz, sbuf, dbuf, dkv):
    blocks = recv_ref.shape[0]
    rows = 128
    half_rows = 64
    tiles = blocks * half_rows // Q_TILE
    per_tile = Q_TILE // half_rows
    half = order_ref[blocks]
    lane = lax.broadcasted_iota(jnp.int32, (half_rows, 128), 1)

    def arrange(b, carry):
        c = order_ref[b]
        kv[pl.ds(pl.multiple_of(b * rows, rows), rows), :] = recv_ref[c, 0:rows, :]
        qg = recv_ref[c, rows : rows + half_rows, :].astype(F32)
        at = pl.ds(pl.multiple_of(b * half_rows, half_rows), half_rows)
        qz[at, :] = jnp.where(lane < HEAD_DIM, qg * (HEAD_DIM**-0.5), 0.0).astype(BF16)
        gz[at, :] = jnp.where(lane < HEAD_DIM, 0.0, qg).astype(BF16)
        return carry

    lax.fori_loop(0, blocks, arrange, 0)

    def turn(j, carry):
        at = pl.ds(pl.multiple_of(j * K_TILE, K_TILE), K_TILE)
        kvt[:, at] = kv[at, :].T
        dkv[at, :] = jnp.zeros((K_TILE, 128), F32)
        return carry

    lax.fori_loop(0, tiles, turn, 0)

    key_row = lax.broadcasted_iota(jnp.int32, (K_TILE, Q_TILE), 0)
    query = lax.broadcasted_iota(jnp.int32, (K_TILE, Q_TILE), 1)
    place = (query // half_rows) * rows + half * half_rows + query % half_rows
    allowed = key_row <= place

    def folded(v, op):
        return op(v.reshape(K_TILE // 8, 8, Q_TILE), axis=0)

    def tile(i, carry):
        q_at = pl.ds(pl.multiple_of(i * Q_TILE, Q_TILE), Q_TILE)
        q = qz[q_at, :]
        g = gz[q_at, :]

        def score(j, top):
            at = pl.ds(pl.multiple_of(j * K_TILE, K_TILE), K_TILE)
            s = dot(kv[at, :], q, 1, 1)
            sbuf[at, :] = s
            return jnp.maximum(top, folded(s, jnp.max))

        top = lax.fori_loop(0, i, score, jnp.full((8, Q_TILE), NEGATIVE, F32))
        last = pl.ds(pl.multiple_of(i * K_TILE, K_TILE), K_TILE)
        s = jnp.where(allowed, dot(kv[last, :], q, 1, 1), NEGATIVE)
        sbuf[last, :] = s
        top = jnp.maximum(top, folded(s, jnp.max))
        top = jnp.max(top, axis=0, keepdims=True)

        def weigh(j, carry):
            total, delta = carry
            at = pl.ds(pl.multiple_of(j * K_TILE, K_TILE), K_TILE)
            p = jnp.exp(sbuf[at, :] - top)
            sbuf[at, :] = p
            dp = dot(kv[at, :], g, 1, 1)
            dbuf[at, :] = dp
            return total + folded(p, jnp.sum), delta + folded(p * dp, jnp.sum)

        zero = jnp.zeros((8, Q_TILE), F32)
        total, delta = lax.fori_loop(0, i + 1, weigh, (zero, zero))
        inverse = 1.0 / jnp.sum(total, axis=0, keepdims=True)
        delta = jnp.sum(delta, axis=0, keepdims=True) * inverse

        def spread(j, carry):
            att, dq = carry
            at = pl.ds(pl.multiple_of(j * K_TILE, K_TILE), K_TILE)
            p = sbuf[at, :] * inverse
            pb = p.astype(BF16)
            ds = (p * (dbuf[at, :] - delta)).astype(BF16)
            kt = kvt[:, at]
            dkv[at, :] = dkv[at, :] + (dot(ds, q) + dot(pb, g))
            return att + dot(kt, pb), dq + dot(kt, ds)

        zeros = jnp.zeros((128, Q_TILE), F32)
        att, dq = lax.fori_loop(0, i + 1, spread, (zeros, zeros))
        feature = lax.broadcasted_iota(jnp.int32, (128, Q_TILE), 0)
        both = jnp.where(feature < HEAD_DIM, dq * (HEAD_DIM**-0.5), att).T.astype(BF16)
        for b in range(per_tile):
            c = order_ref[i * per_tile + b]
            out_ref[c, rows : rows + half_rows, :] = both[b * half_rows : (b + 1) * half_rows, :]
        return carry

    lax.fori_loop(0, tiles, tile, 0)

    def put(b, carry):
        c = order_ref[b]
        at = pl.ds(pl.multiple_of(b * rows, rows), rows)
        out_ref[c, 0:rows, :] = dkv[at, :].astype(BF16)
        return carry

    lax.fori_loop(0, blocks, put, 0)


def attention(order, received):
    blocks = received.shape[0]
    keys = blocks * 128
    queries = blocks * 64
    return pl.pallas_call(
        attention_kernel,
        grid_spec=pltpu.PrefetchScalarGridSpec(
            num_scalar_prefetch=1,
            grid=(),
            in_specs=[pl.BlockSpec(memory_space=pltpu.VMEM)],
            out_specs=pl.BlockSpec(memory_space=pltpu.VMEM),
            scratch_shapes=[
                pltpu.VMEM((keys, 128), BF16),
                pltpu.VMEM((128, keys), BF16),
                pltpu.VMEM((queries, 128), BF16),
                pltpu.VMEM((queries, 128), BF16),
                pltpu.VMEM((keys, Q_TILE), F32),
                pltpu.VMEM((keys, Q_TILE), F32),
                pltpu.VMEM((keys, 128), F32),
            ],
        ),
        out_shape=jax.ShapeDtypeStruct(received.shape, BF16),
        compiler_params=pltpu.CompilerParams(vmem_limit_bytes=40 * 1024 * 1024),
        cost_estimate=pl.CostEstimate(
            flops=keys * queries * 64 * 6, bytes_accessed=2 * received.size * 2, transcendentals=keys * queries // 2
        ),
    )(order, received)


def swap(value, flip):
    return lax.ppermute(value, "fsdp", [(i, i ^ flip) for i in range(4)])


def shuffle(chunk_of, mine):
    own = chunk_of(mine)
    whole = jnp.zeros((4,) + own.shape, own.dtype)
    for flip in range(4):
        other = mine ^ flip
        piece = own if flip == 0 else swap(chunk_of(other), flip)
        whole = lax.dynamic_update_slice(whole, piece[None], (other, 0, 0))
    return whole.reshape(4 * own.shape[0], own.shape[1])


def on_device(
    tokens,
    block_order,
    weight_qkv,
    bias_qkv,
    weight_dense,
    bias_dense,
    weight_up,
    bias_up,
    weight_down,
    bias_down,
    gain_one,
    shift_one,
    gain_two,
    shift_two,
    cotangent,
):
    rows = tokens.shape[2]
    width = tokens.shape[3]
    blocks = lax.axis_size("ctx")
    ctx = lax.axis_index("ctx")
    mine = lax.axis_index("fsdp")
    part = width // 4
    own_tokens = tokens.reshape(rows, width)
    own_cot = cotangent.reshape(rows, width)

    def gather(value):
        across = swap(value, 2)
        return [value, swap(value, 1), across, swap(across, 1)]

    vectors = jnp.concatenate(
        [gain_one, shift_one, gain_two, shift_two, bias_dense, bias_down, bias_qkv, jnp.zeros((768,), BF16)]
    ).reshape(3, width)
    packed = gather(jnp.concatenate([own_tokens, vectors, jnp.zeros((13, width), BF16)], axis=0))
    four_tokens = jnp.concatenate([piece[:rows] for piece in packed], axis=0)
    natural = jnp.arange(4) ^ mine
    vectors = jnp.stack([piece[rows : rows + 3] for piece in packed])[natural].reshape(4, 3 * width)

    def whole_vector(at, size=part):
        return vectors[:, at : at + size].reshape(4 * size).astype(F32)

    gone, sone, gtwo, stwo, bdense, bdown = [whole_vector(part * i) for i in range(6)]
    bqkv = lax.dynamic_slice_in_dim(whole_vector(6 * part, 768).reshape(3, 4, part), mine, 1, axis=1).reshape(768)

    def qkv_chunk(j):
        return jnp.concatenate(
            [lax.dynamic_slice_in_dim(weight_qkv, width * i + part * j, part, axis=1) for i in range(3)], axis=1
        )

    my_qkv = shuffle(qkv_chunk, mine)
    four_cot = jnp.concatenate(gather(own_cot), axis=0)
    my_up = shuffle(lambda j: lax.dynamic_slice_in_dim(weight_up, width * j, width, axis=1), mine)
    my_down = shuffle(lambda j: lax.dynamic_slice_in_dim(weight_down, width * j, width, axis=1), mine)

    inputs = four_tokens.astype(F32)
    centre = inputs - jnp.mean(inputs, axis=-1, keepdims=True)
    spread = lax.rsqrt(jnp.mean(centre * centre, axis=-1, keepdims=True) + EPSILON)
    normal = centre * spread
    low_one = (normal * gone + sone).astype(BF16)
    low_two = (normal * gtwo + stwo).astype(BF16)

    places = (block_order[ctx] * rows + jnp.arange(rows, dtype=jnp.int32)).astype(F32)
    halfway = ROT_DIMS // 2
    inverse = 10000.0 ** (-2.0 * jnp.arange(halfway).astype(F32) / ROT_DIMS)
    phases = places[:, None] * inverse[None, :]
    cos8, sin8 = jnp.cos(phases), jnp.sin(phases)
    zero8 = jnp.zeros_like(sin8)
    rest = jnp.zeros((rows, HEAD_DIM - ROT_DIMS), F32)
    cos_all = jnp.tile(jnp.concatenate([cos8, cos8, rest + 1.0], axis=1), (4, 4))
    sin_low = jnp.tile(jnp.concatenate([-sin8, zero8, rest], axis=1), (4, 4))
    sin_high = jnp.tile(jnp.concatenate([zero8, sin8, rest], axis=1), (4, 4))

    def turn(u, sign):
        return u * cos_all + sign * (
            jnp.roll(u, -halfway, axis=1) * sin_low + jnp.roll(u, halfway, axis=1) * sin_high
        )

    projected = dot(low_one, my_qkv) + bqkv
    queries = turn(projected[:, :part], 1.0).astype(BF16)
    key_rows = turn(projected[:, part : 2 * part], 1.0).astype(BF16)
    values = projected[:, 2 * part :].astype(BF16)
    grad_att = dot(four_cot, weight_dense, 1, 1).astype(BF16)

    def by_head(value):
        return value.reshape(4, rows, 4, HEAD_DIM).transpose(0, 2, 1, 3)

    kv = jnp.concatenate([by_head(key_rows), by_head(values)], axis=-1)
    qg = jnp.concatenate([by_head(queries), by_head(grad_att)], axis=-1).reshape(4, 4, 2, rows // 2, 128)
    message = jnp.concatenate([jnp.broadcast_to(kv[:, :, None], (4, 4, 2, rows, 128)), qg], axis=3)
    received = lax.all_to_all(message.reshape(blocks, 192, 128), "ctx", 0, 0, tiled=True)
    order = jnp.zeros((blocks,), jnp.int32).at[block_order].set(jnp.arange(blocks, dtype=jnp.int32))
    order = jnp.concatenate([order, (ctx % 2).astype(jnp.int32)[None]])
    answer = attention(order, received)
    back = lax.all_to_all(answer, "ctx", 0, 0, tiled=True).reshape(4, 4, 2, 192, 128)

    upward = dot(low_two, my_up) + bias_up.astype(F32)
    activated, gelu_back = jax.vjp(lambda v: jax.nn.gelu(v, approximate=False), upward)
    act_low = activated.astype(BF16)
    grad_act = dot(four_cot, my_down)
    grad_up = gelu_back(grad_act)[0].astype(BF16)
    mlp_out = dot(act_low, my_down, 1, 1)
    grad_two = dot(grad_up, my_up, 1, 1)
    gup = dot(low_two, grad_up, 0, 0)
    gdown = dot(four_cot, act_low, 0, 0)

    dkv = jnp.sum(back[:, :, :, :rows].astype(F32), axis=2)
    qa = back[:, :, :, rows:].reshape(4, 4, rows, 128)

    def by_token(value):
        return value.transpose(0, 2, 1, 3).reshape(4 * rows, part)

    att = by_token(qa[..., HEAD_DIM:])
    grad_qkv = jnp.concatenate(
        [
            turn(by_token(qa[..., :HEAD_DIM]).astype(F32), -1.0),
            turn(by_token(dkv[..., :HEAD_DIM]), -1.0),
            by_token(dkv[..., HEAD_DIM:]),
        ],
        axis=1,
    ).astype(BF16)
    grad_one = dot(grad_qkv, my_qkv, 1, 1)
    gqkv = dot(low_one, grad_qkv, 0, 0)
    gdense = dot(att, four_cot, 0, 0)

    def norm_back(grad, gain):
        e = grad * gain
        return spread * (
            e - jnp.mean(e, axis=-1, keepdims=True) - normal * jnp.mean(e * normal, axis=-1, keepdims=True)
        )

    out_part = mlp_out + dot(att, weight_dense)
    in_part = norm_back(grad_one, gone) + norm_back(grad_two, gtwo)

    def collect(partial):
        low = partial.astype(BF16)
        total = partial[:rows]
        for flip in range(1, 4):
            total = total + swap(low[flip * rows : (flip + 1) * rows], flip).astype(F32)
        return total

    both = collect(jnp.concatenate([out_part, in_part], axis=1))
    out_block = (own_tokens.astype(F32) + both[:, :width] + (bdense + bdown)).astype(BF16)
    grad_tokens = (own_cot.astype(F32) + both[:, width:]).astype(BF16)

    def owners(value):
        return value.reshape(4, blocks, 8, value.shape[1]).transpose(1, 0, 2, 3).astype(BF16)

    cot32 = four_cot.astype(F32)
    sum_cot = lax.dynamic_slice_in_dim(jnp.sum(cot32, axis=0), mine * part, part)
    norms = jnp.stack(
        [
            jnp.sum(grad_one * normal, axis=0),
            jnp.sum(grad_one, axis=0),
            jnp.sum(grad_two * normal, axis=0),
            jnp.sum(grad_two, axis=0),
        ]
    )
    norms = norms.reshape(4, 4, blocks, 8).transpose(2, 1, 0, 3).reshape(blocks, 4, 32)
    sum_qkv = jnp.sum(grad_qkv.astype(F32), axis=0).reshape(blocks, 1, 24)
    sum_up = jnp.sum(grad_up.astype(F32), axis=0).reshape(blocks, 4, 8)
    small = jnp.concatenate(
        [
            norms,
            jnp.broadcast_to(sum_qkv, (blocks, 4, 24)),
            sum_up,
            sum_cot.reshape(blocks, 4, 2),
            jnp.zeros((blocks, 4, 62), F32),
        ],
        axis=2,
    )
    small = jnp.pad(small[:, :, None, :], ((0, 0), (0, 0), (0, 7), (0, 0))).astype(BF16)
    dense_piece = gdense.reshape(blocks, 8, 4, part).transpose(0, 2, 1, 3).astype(BF16)
    outgoing = jnp.concatenate([owners(gqkv), owners(gup), owners(gdown), dense_piece, small], axis=3)
    arrived = lax.all_to_all(outgoing, "ctx", 0, 0, tiled=True)
    summed = jnp.sum(arrived.astype(F32), axis=0).astype(BF16)
    crossed = lax.all_to_all(summed, "fsdp", 0, 0, tiled=True)
    up_at, down_at, dense_at, small_at = 768, 768 + width, 768 + 2 * width, 1024 + 2 * width
    mat_qkv = crossed[:, :, :768].reshape(4, 8, 3, part).transpose(1, 2, 0, 3).reshape(8, 3 * width)
    mat_up = crossed[:, :, up_at:down_at].transpose(1, 0, 2).reshape(8, 4 * width)
    mat_down = crossed[:, :, down_at:dense_at].transpose(1, 0, 2).reshape(8, 4 * width)
    mat_dense = summed[:, :, dense_at:small_at].transpose(1, 0, 2).reshape(8, width)
    vec_norm = jnp.sum(crossed[:, 0, small_at : small_at + 32].astype(F32), axis=0).astype(BF16)
    vec_qkv = crossed[:, 0, small_at + 32 : small_at + 56].reshape(96)
    vec_up = summed[:, 0, small_at + 56 : small_at + 64].reshape(32)
    vec_cot = summed[:, 0, small_at + 64 : small_at + 66].reshape(8)
    vec = jnp.concatenate([vec_norm, vec_qkv, vec_up, vec_cot, jnp.zeros((88,), BF16)])
    vec = jnp.pad(vec[None], ((0, 7), (0, 0)))
    chunk = jnp.concatenate([mat_qkv, mat_dense, mat_up, mat_down, vec], axis=1)
    full = lax.all_to_all(jnp.broadcast_to(chunk[None], (blocks,) + chunk.shape), "ctx", 0, 0, tiled=True)
    full = full.reshape(blocks * 8, chunk.shape[1])

    def columns(at, size):
        return full[:, at : at + size].astype(F32)

    g_qkv = columns(0, 3 * width)
    g_dense = columns(3 * width, width)
    g_up = columns(4 * width, 4 * width)
    g_down = columns(8 * width, 4 * width)
    vec = full.reshape(blocks, 8, chunk.shape[1])[:, 0, 12 * width :].astype(F32)
    g_norm = vec[:, :32].reshape(blocks, 4, 8).transpose(1, 0, 2).reshape(4, part)
    g_bqkv = vec[:, 32:128].reshape(blocks, 4, 24).transpose(1, 0, 2).reshape(4, 3, part)
    g_bqkv = lax.dynamic_slice_in_dim(g_bqkv.transpose(1, 0, 2).reshape(3 * width), mine * 768, 768)
    g_bup = vec[:, 128:160].reshape(width)
    g_cot = vec[:, 160:168].reshape(part)
    return (
        out_block.reshape(tokens.shape),
        grad_tokens.reshape(tokens.shape),
        g_qkv,
        g_bqkv,
        g_dense,
        g_cot,
        g_up,
        g_bup,
        g_down,
        g_cot,
        g_norm[0],
        g_norm[1],
        g_norm[2],
        g_norm[3],
    )


def solution(mesh):
    block = P("ctx", "fsdp", None, None)
    matrix = P("fsdp", None)
    vector = P("fsdp")
    return jax.shard_map(
        on_device,
        mesh=mesh,
        in_specs=(
            block,
            P(),
            matrix,
            vector,
            matrix,
            vector,
            matrix,
            vector,
            matrix,
            vector,
            vector,
            vector,
            vector,
            vector,
            block,
        ),
        out_specs=(
            block,
            block,
            matrix,
            vector,
            matrix,
            vector,
            matrix,
            vector,
            matrix,
            vector,
            vector,
            vector,
            vector,
            vector,
        ),
        check_vma=False,
    )
```

time: 1680 us -> 507 us (0.30)
  waiting for transfers between devices: 1170 us -> 165 us
  matrix products: 228 us -> 43.6 us
  starting transfers between devices: 0.9 us -> 46.3 us
  blocking collectives: 124 us -> 81.1 us
  Pallas kernels: 0 us -> 36.2 us
    reduce_scatter x6 -> x0, waiting for transfers between devices: 563 us -> none  [the longest x1 176 us: on_device(): lax.psum_scatter(grad_value_all.reshape(length, model_width).astype(jnp.b...]
    all_gather x6 -> x0, waiting for transfers between devices: 372 us -> none  [the longest x1 168 us: on_device(): lax.all_gather(key_rows.reshape(rows_here, model_width), 'ctx', axis=0, t...]
    psum x1 -> x0, waiting for transfers between devices: 229 us -> none  [on_device(): lax.psum(mat_down.astype(jnp.bfloat16), 'ctx').astype(jnp.float32)]
    dot_general x68 -> x12, matrix products: 228 us -> 43.6 us  [dot(): lax.dot_general(a, b, (((ca,), (cb,)), ((), ())), preferred_element_type=...]
    ppermute x0 -> x18, waiting for transfers between devices: none -> 144 us  [swap(): return lax.ppermute(value, 'fsdp', [(i, i ^ flip) for i in range(4)])]
    all_to_all x0 -> x1, blocking collectives: none -> 81.1 us  [on_device(): arrived = lax.all_to_all(outgoing, 'ctx', 0, 0, tiled=True)]
    psum x1 -> x0, blocking collectives: 71.6 us -> none  [on_device(): vector_total = lax.psum(vector_parts, ('ctx', 'fsdp'))]
    all_gather x8 -> x0, blocking collectives: 52.8 us -> none  [the longest x1 6.67 us: on_device(): lax.all_gather(bias_qkv, 'fsdp', axis=0, tiled=True)]
  transfers between devices with their start and end apart: 13 -> 22, of which waited for: 11 -> 10; matrix products, arithmetic and copies ran while one was open for 21% -> 16% of each run, Pallas kernels for 0% -> 0%
where the time goes in v1:
time: 507 us; the launch traced here: 498 us
  waiting for transfers between devices  165 us (33%)
  local copies, waits for them, and re-layouts  81.9 us (16%)
  blocking collectives  81.1 us (16%)
  starting transfers between devices  46.3 us (9%)
  matrix products  43.6 us (9%)
  other arithmetic  41.3 us (8%)
  Pallas kernels  36.2 us (7%)
    ppermute x18, waiting for transfers between devices, swap(): return lax.ppermute(value, 'fsdp', [(i, i ^ flip) for i in range(4)])  144 us
    all_to_all x1, blocking collectives, on_device(): arrived = lax.all_to_all(outgoing, 'ctx', 0, 0, tiled=True)  81.1 us
    dot_general x12, matrix products, dot(): lax.dot_general(a, b, (((ca,), (cb,)), ((), ())), preferred_element_type=...  43.6 us
    pallas_call x1, Pallas kernels, attention(): pl.pallas_call(attention_kernel, grid_spec=pltpu.PrefetchScalarGridSpec(n...  36.2 us
    ppermute x18, starting transfers between devices, swap(): return lax.ppermute(value, 'fsdp', [(i, i ^ flip) for i in range(4)])  20.3 us
    unnamed x156, local copies, waits for them, and re-layouts  19.8 us
    all_to_all x1, waiting for transfers between devices, on_device(): lax.all_to_all(message.reshape(blocks, 192, 128), 'ctx', 0, 0, tiled=True)  12.9 us
    convert_element_type x3, other arithmetic, columns(): return full[:, at:at + size].astype(F32)  12.3 us
  transfers between devices with their start and end apart: 22, of which 10 were waited for; matrix products, arithmetic and copies ran while one was open for 16% of the time, Pallas kernels for 0%

profile of v1, /device:TPU:2, one launch (start us, length us, event | category | flops | bytes accessed | tf_op | source)
XLA Modules:
  0.0 498.1 jit_solution(9511773015766844792)
XLA Ops:
  0.7 2.2 collective-permute-start.13
  9.0 1.8 maximum_maximum_fusion
  10.8 1.4 collective-permute-start.1
  12.4 2.4 constant_dynamic-slice_fusion.3
  22.8 2.0 copy.203
  26.2 1.6 broadcast.126.clone.1
  31.2 2.1 collective-permute-start.10
  39.4 5.3 %collective-permute-done.10 = bf16[256,768]{1,0:T(8,128)(2,1)S(1)} collective-permute-done((bf16[256,768]{1,0:T(8,128)(2,1)S(1)}, bf16[256,768]{1,0:T(8,128)(2,1)S(1)}, u32[]{:S(2)}, u32[]{:S(2)}) %collective-permute-start.10) | collective-permute-done | bytes 393248 | tf_op jit(solution)/shard_map/ppermute | solution.py:152
  44.6 2.1 collective-permute-start.7
  46.8 4.8 collective-permute-done.11
  51.6 1.2 collective-permute-start.3
  52.9 1.8 collective-permute-start.8
  54.8 1.5 collective-permute-start.4
  56.3 8.0 %collective-permute-done.7 = bf16[256,1024]{1,0:T(8,128)(2,1)S(1)} collective-permute-done((bf16[256,1024]{1,0:T(8,128)(2,1)S(1)}, bf16[256,1024]{1,0:T(8,128)(2,1)S(1)}, u32[]{:S(2)}, u32[]{:S(2)}) %collective-permute-start.7) | collective-permute-done | bytes 524320 | tf_op jit(solution)/shard_map/ppermute | solution.py:152
  64.4 2.3 collective-permute-start.5
  67.7 2.3 convolution_convert_fusion.4
  71.1 15.6 %collective-permute-done.4 = bf16[256,1024]{1,0:T(8,128)(2,1)S(1)} collective-permute-done((bf16[256,1024]{1,0:T(8,128)(2,1)S(1)}, bf16[256,1024]{1,0:T(8,128)(2,1)S(1)}, u32[]{:S(2)}, u32[]{:S(2)}) %collective-permute-start.4) | collective-permute-done | bytes 524320 | tf_op jit(solution)/shard_map/ppermute | solution.py:152
  87.6 1.2 convert_reduce_fusion.1
  90.7 1.3 copy.236
  92.9 3.8 collective-permute-done.5
  96.7 2.2 bitcast_dynamic-update-slice_fusion.3
  102.1 2.5 convolution_add_fusion.1
  106.3 1.4 fusion.43
  107.7 1.1 copy.210
  108.9 1.3 pad_maximum_fusion.6
  112.9 2.4 pad_maximum_fusion.1
  115.2 9.6 %all-to-all-start = ((bf16[32,192,128]{2,1,0:T(8,128)(2,1)}), bf16[32,192,128]{2,1,0:T(8,128)(2,1)S(1)}, u32[]{:S(2)}, u32[]{:S(2)}) async-start(bf16[32,192,128]{2,1,0:T(8,128)(2,1)} %pad_maximum_fusion.1), calls=%async_computation | async-start | bytes 3145728 | tf_op jit(solution)/shard_map/all_to_all | solution.py:254
  124.8 9.6 %multiply_convert_fusion = (bf16[512,1024]{1,0:T(8,128)(2,1)}, f32[512,1024]{1,0:T(8,128)}, f32[512,1024]{1,0:T(8,128)}) fusion(f32[1024]{0:T(1024)S(1)} %convert_element_type.218, bf16[1024,1024]{1,0:T(8,128)(2,1)} %bitcast.9, f32[1024]{0:T(1024)S(1)} %bitcast.307, f32[1024]{0:T(1024)S(1)} %bitcast.300, f32[512]{0:T(512)S(1)} %add_rsqrt_fusion, ...), kind=kOutput, calls=%fused_computation.40 | convolution fusion | flops 1115160576 | bytes 8404992 | tf_op jit(solution)/shard_map/dot_general | solution.py:21
  134.5 12.9 %all-to-all-done.recv_ref = bf16[32,192,128]{2,1,0:T(8,128)(2,1)S(1)} async-done(((bf16[32,192,128]{2,1,0:T(8,128)(2,1)}), bf16[32,192,128]{2,1,0:T(8,128)(2,1)S(1)}, u32[]{:S(2)}, u32[]{:S(2)}) %all-to-all-start) | async-done | bytes 1572896 | tf_op jit(solution)/shard_map/all_to_all | solution.py:254
  147.4 36.2 %shard_map.254 = bf16[32,192,128]{2,1,0:T(8,128)(2,1)} custom-call(s32[33]{0:T(128)S(1)} %pad_add_fusion.order_ref, bf16[32,192,128]{2,1,0:T(8,128)(2,1)S(1)} %all-to-all-done.recv_ref), custom_call_target="tpu_custom_call" | custom-call | flops 3221225472 | bytes 3145728 | tf_op jit(solution)/shard_map/pallas_call | solution.py:126
  183.6 6.2 %all-to-all-start.1 = ((bf16[32,192,128]{2,1,0:T(8,128)(2,1)}), bf16[32,192,128]{2,1,0:T(8,128)(2,1)S(1)}, u32[]{:S(2)}, u32[]{:S(2)}) async-start(bf16[32,192,128]{2,1,0:T(8,128)(2,1)} %shard_map.254), calls=%async_computation.1 | async-start | bytes 3145728 | tf_op jit(solution)/shard_map/all_to_all | solution.py:258
  189.8 6.1 %fusion.86 = (bf16[1024]{0:T(1024)(128)(2,1)S(1)}, bf16[512,1024]{1,0:T(8,128)(2,1)}) fusion(f32[512,1024]{1,0:T(8,128)} %get-tuple-element.23, bf16[1024,1024]{1,0:T(8,128)(2,1)} %bitcast.256, bf16[128,1024]{1,0:T(8,128)(2,1)} %copy-done.43, bf16[128,1024]{1,0:T(8,128)(2,1)} %collective-permute-done.13, bf16[128,1024]{1,0:T(8,128)(2,1)} %collective-permute-done.12, ...), kind=kOutput, calls=%fused_computation.224 | convolution fusion | flops 1086323712 | bytes 8394752 | tf_op jit(solution)/shard_map/dot_general | solution.py:21
  196.6 4.3 convolution_convert_fusion
  200.9 4.3 fusion.87
  205.2 2.8 convolution_convert_fusion.1
  208.0 3.2 all-to-all-done.1
  211.2 1.1 copy-done.3
  212.4 1.5 convert_reduce_fusion.2
  213.9 1.4 convert_bitcast_fusion
  215.3 1.6 copy.214
  220.1 1.6 copy.215
  222.9 2.0 copy.216
  225.9 2.2 fusion.49
  228.2 2.5 convolution_convert_fusion.2
  231.8 6.2 %fusion.21 = (bf16[1024]{0:T(1024)(128)(2,1)S(1)}, f32[512]{0:T(512)}, f32[512]{0:T(512)}, bf16[1024]{0:T(1024)(128)(2,1)S(1)}, bf16[1024]{0:T(1024)(128)(2,1)S(...) fusion(f32[512]{0:T(512)S(1)} %add_rsqrt_fusion, ...), kind=kOutput, calls=%fused_computation.29 | convolution fusion | flops 820242432 | bytes 7630848 | tf_op jit(solution)/shard_map/dot_general | solution.py:21
  238.0 1.5 bitcast_dynamic-update-slice_fusion.2
  246.0 1.6 bitcast_dynamic-update-slice_fusion.1
  248.4 1.5 bitcast_dynamic-update-slice_fusion
  250.1 1.3 fusion.31
  252.2 81.1 %all_to_all.25 = bf16[32,4,8,3200]{3,2,1,0:T(8,128)(2,1)} all-to-all(bf16[32,4,8,3200]{3,2,1,0:T(8,128)(2,1)} %pad_dynamic-update-slice_fusion), channel_id=1, replica_groups=mesh['ctx'=32,'fsdp'=4] {'ctx'}, dimensions={0} | all-to-all | bytes 13107200 | tf_op jit(solution)/shard_map/all_to_all | solution.py:338
  333.3 4.7 reduce_sum.164
  338.0 3.4 all-to-all-start.3
  343.9 4.4 all-to-all-done.3
  348.8 3.1 broadcast_in_dim.132
  352.0 6.8 %all-to-all-start.4 = ((bf16[32,8,12544]{2,1,0:T(8,128)(2,1)}), bf16[32,8,12544]{2,1,0:T(8,128)(2,1)}, u32[]{:S(2)}, u32[]{:S(2)}) async-start(bf16[32,8,12544]{2,1,0:T(8,128)(2,1)} %broadcast_in_dim.132), calls=%async_computation.4 | async-start | bytes 12845056 | tf_op jit(solution)/shard_map/all_to_all | solution.py:353
  360.4 1.3 convolution_add_fusion
  362.7 1.7 fusion.18
  365.8 2.5 collective-permute-start.16
  369.9 94.2 %collective-permute-done.17 = bf16[128,2048]{1,0:T(8,128)(2,1)} collective-permute-done((bf16[128,2048]{1,0:T(8,128)(2,1)}, bf16[128,2048]{1,0:T(8,128)(2,1)}, u32[]{:S(2)}, u32[]{:S(2)}) %collective-permute-start.17) | collective-permute-done | bytes 524320 | tf_op jit(solution)/shard_map/ppermute | solution.py:152
  464.1 12.2 %collective-permute-done.16 = bf16[128,2048]{1,0:T(8,128)(2,1)} collective-permute-done((bf16[128,2048]{1,0:T(8,128)(2,1)}, bf16[128,2048]{1,0:T(8,128)(2,1)}, u32[]{:S(2)}, u32[]{:S(2)}) %collective-permute-start.16) | collective-permute-done | bytes 524320 | tf_op jit(solution)/shard_map/ppermute | solution.py:152
  476.3 1.8 fusion.35
  479.1 3.4 slice_convert_fusion.2
  482.5 2.1 slice_convert_fusion.4
  485.7 6.7 %slice_convert_fusion = (f32[256,4096]{1,0:T(8,128)}, f32[256,4096]{1,0:T(8,128)}) fusion(bf16[256,12544]{1,0:T(8,128)(2,1)} %bitcast.61), kind=kLoop, calls=%fused_computation.33 | loop fusion | flops 2097152 | bytes 12582912 | tf_op jit(solution)/shard_map/convert_element_type | solution.py:357
  (324 shorter events, 68.6 us)
Async XLA Ops:
  0.6 67.0 %copy-start = (bf16[256,1024]{1,0:T(8,128)(2,1)S(1)}, bf16[256,1024]{1,0:T(8,128)(2,1)}, u32[]{:S(2)}) copy-start(bf16[256,1024]{1,0:T(8,128)(2,1)} %param.19) | copy-start | bytes 1572868
  0.7 54.1 %collective-permute-start.13 = (bf16[128,1024]{1,0:T(8,128)(2,1)}, bf16[128,1024]{1,0:T(8,128)(2,1)}, u32[]{:S(2)}, u32[]{:S(2)}) collective-permute-start(bf16[128,1024]{1,0:T(8,128)(2,1)} %bitcast.249), channel_id=1, source_target_pairs={{0,2},{1,3},{2,0},{3,1},{4,6},{5,7},{6,4},{7,5},{8,10},{9,11},{10,... | collective-permute-start | bytes 786440 | tf_op jit(solution)/shard_map/ppermute | solution.py:152
  2.9 64.6 %collective-permute-start.12 = (bf16[128,1024]{1,0:T(8,128)(2,1)}, bf16[128,1024]{1,0:T(8,128)(2,1)}, u32[]{:S(2)}, u32[]{:S(2)}) collective-permute-start(bf16[128,1024]{1,0:T(8,128)(2,1)} %bitcast.250), channel_id=1, source_target_pairs={{0,1},{1,0},{2,3},{3,2},{4,5},{5,4},{6,7},{7,6},{8,9},{9,8},{10,11... | collective-permute-start | bytes 786440 | tf_op jit(solution)/shard_map/ppermute | solution.py:152
  10.8 5.1 %copy-start.60 = (s32[32]{0:T(128)S(1)}, s32[32]{0:T(128)}, u32[]{:S(2)}) copy-start(s32[32]{0:T(128)} %param.16) | copy-start | bytes 388
  10.8 20.4 %collective-permute-start.1 = (bf16[144,1024]{1,0:T(8,128)(2,1)}, bf16[144,1024]{1,0:T(8,128)(2,1)}, u32[]{:S(2)}, u32[]{:S(2)}) collective-permute-start(bf16[144,1024]{1,0:T(8,128)(2,1)} %maximum_maximum_fusion), channel_id=1, source_target_pairs={{0,2},{1,3},{2,0},{3,1},{4,6},{5,7},{6,4},{7,5},{8,10},{9,11},{10,... | collective-permute-start | bytes 884744 | tf_op jit(solution)/shard_map/ppermute | solution.py:152
  12.2 22.1 %collective-permute-start = (bf16[144,1024]{1,0:T(8,128)(2,1)}, bf16[144,1024]{1,0:T(8,128)(2,1)}, u32[]{:S(2)}, u32[]{:S(2)}) collective-permute-start(bf16[144,1024]{1,0:T(8,128)(2,1)} %maximum_maximum_fusion), channel_id=1, source_target_pairs={{0,1},{1,0},{2,3},{3,2},{4,5},{5,4},{6,7},{7,6},{8,9},{9,8},{10,11... | collective-permute-start | bytes 884744 | tf_op jit(solution)/shard_map/ppermute | solution.py:152
  15.6 22.2 %collective-permute-start.9 = (bf16[256,768]{1,0:T(8,128)(2,1)}, bf16[256,768]{1,0:T(8,128)(2,1)}, u32[]{:S(2)}, u32[]{:S(2)}) collective-permute-start(bf16[256,768]{1,0:T(8,128)(2,1)} %pad_maximum_fusion.7), channel_id=1, source_target_pairs={{0,1},{1,0},{2,3},{3,2},{4,5},{5,4},{6,7},{7,6},{8,9},{9,8},{10,11... | collective-permute-start | bytes 1179656 | tf_op jit(solution)/shard_map/ppermute | solution.py:152
  20.1 4.8 copy-start.55
  22.0 4.0 copy-start.24
  26.0 3.0 copy-start.48
  26.1 3.0 copy-start.49
  26.1 3.0 copy-start.50
  26.1 2.9 copy-start.45
  26.1 2.9 copy-start.46
  26.1 2.9 copy-start.47
  31.2 13.5 %collective-permute-start.10 = (bf16[256,768]{1,0:T(8,128)(2,1)S(1)}, bf16[256,768]{1,0:T(8,128)(2,1)S(1)}, u32[]{:S(2)}, u32[]{:S(2)}) collective-permute-start(bf16[256,768]{1,0:T(8,128)(2,1)S(1)} %pad_maximum_fusion.8), channel_id=1, source_target_pairs={{0,2},{1,3},{2,0},{3,1},{4,6},{5,7},{6,4},{7,5},{8,10},{9,11},{10,... | collective-permute-start | bytes 1179656 | tf_op jit(solution)/shard_map/ppermute | solution.py:152
  34.3 170.9 %copy-start.8 = (bf16[128,1024]{1,0:T(8,128)(2,1)}, bf16[128,1024]{1,0:T(8,128)(2,1)S(1)}, u32[]{:S(2)}) copy-start(bf16[128,1024]{1,0:T(8,128)(2,1)S(1)} %slice.281) | copy-start | bytes 786436
  34.3 17.4 %collective-permute-start.11 = (bf16[256,768]{1,0:T(8,128)(2,1)S(1)}, bf16[256,768]{1,0:T(8,128)(2,1)S(1)}, u32[]{:S(2)}, u32[]{:S(2)}) collective-permute-start(bf16[256,768]{1,0:T(8,128)(2,1)S(1)} %pad_maximum_fusion.9), channel_id=1, source_target_pairs={{0,3},{1,2},{2,1},{3,0},{4,7},{5,6},{6,5},{7,4},{8,11},{9,10},{10,... | collective-permute-start | bytes 1179656 | tf_op jit(solution)/shard_map/ppermute | solution.py:152
  36.3 65.8 %copy-start.11 = (bf16[128,1024]{1,0:T(8,128)(2,1)}, bf16[128,1024]{1,0:T(8,128)(2,1)S(1)}, u32[]{:S(2)}) copy-start(bf16[128,1024]{1,0:T(8,128)(2,1)S(1)} %slice.280) | copy-start | bytes 786436
  37.8 15.1 %collective-permute-start.6 = (bf16[256,1024]{1,0:T(8,128)(2,1)S(1)}, bf16[256,1024]{1,0:T(8,128)(2,1)S(1)}, u32[]{:S(2)}, u32[]{:S(2)}) collective-permute-start(bf16[256,1024]{1,0:T(8,128)(2,1)S(1)} %get-tuple-element.32), channel_id=1, source_target_pairs={{0,1},{1,0},{2,3},{3,2},{4,5},{5,4},{6,7},{7,6},{8,9},{9,8},{10,11... | collective-permute-start | bytes 1572872 | tf_op jit(solution)/shard_map/ppermute | solution.py:152
  44.6 19.7 %collective-permute-start.7 = (bf16[256,1024]{1,0:T(8,128)(2,1)S(1)}, bf16[256,1024]{1,0:T(8,128)(2,1)S(1)}, u32[]{:S(2)}, u32[]{:S(2)}) collective-permute-start(bf16[256,1024]{1,0:T(8,128)(2,1)S(1)} %get-tuple-element.33), channel_id=1, source_target_pairs={{0,2},{1,3},{2,0},{3,1},{4,6},{5,7},{6,4},{7,5},{8,10},{9,11},{10,... | collective-permute-start | bytes 1572872 | tf_op jit(solution)/shard_map/ppermute | solution.py:152
  46.8 20.9 %copy-start.20 = (bf16[1,1,128,1024]{3,2,1,0:T(8,128)(2,1)S(1)}, bf16[1,1,128,1024]{3,2,1,0:T(8,128)(2,1)}, u32[]{:S(2)}) copy-start(bf16[1,1,128,1024]{3,2,1,0:T(8,128)(2,1)} %param.29) | copy-start | bytes 786436
  51.6 12.7 %collective-permute-start.3 = (bf16[256,1024]{1,0:T(8,128)(2,1)S(1)}, bf16[256,1024]{1,0:T(8,128)(2,1)S(1)}, u32[]{:S(2)}, u32[]{:S(2)}) collective-permute-start(bf16[256,1024]{1,0:T(8,128)(2,1)S(1)} %get-tuple-element.35), channel_id=1, source_target_pairs={{0,1},{1,0},{2,3},{3,2},{4,5},{5,4},{6,7},{7,6},{8,9},{9,8},{10,11... | collective-permute-start | bytes 1572872 | tf_op jit(solution)/shard_map/ppermute | solution.py:152
  52.9 14.8 %copy-start.35 = (bf16[4,256,768]{2,1,0:T(8,128)(2,1)}, bf16[4,256,768]{2,1,0:T(8,128)(2,1)S(1)}, u32[]{:S(2)}) copy-start(bf16[4,256,768]{2,1,0:T(8,128)(2,1)S(1)} %bitcast_dynamic-update-slice_fusion.11) | copy-start | bytes 4718596
  52.9 39.9 %collective-permute-start.8 = (bf16[256,1024]{1,0:T(8,128)(2,1)}, bf16[256,1024]{1,0:T(8,128)(2,1)}, u32[]{:S(2)}, u32[]{:S(2)}) collective-permute-start(bf16[256,1024]{1,0:T(8,128)(2,1)} %get-tuple-element.31), channel_id=1, source_target_pairs={{0,3},{1,2},{2,1},{3,0},{4,7},{5,6},{6,5},{7,4},{8,11},{9,10},{10,... | collective-permute-start | bytes 1572872 | tf_op jit(solution)/shard_map/ppermute | solution.py:152
  54.8 32.0 %collective-permute-start.4 = (bf16[256,1024]{1,0:T(8,128)(2,1)S(1)}, bf16[256,1024]{1,0:T(8,128)(2,1)S(1)}, u32[]{:S(2)}, u32[]{:S(2)}) collective-permute-start(bf16[256,1024]{1,0:T(8,128)(2,1)S(1)} %get-tuple-element.36), channel_id=1, source_target_pairs={{0,2},{1,3},{2,0},{3,1},{4,6},{5,7},{6,4},{7,5},{8,10},{9,11},{10,... | collective-permute-start | bytes 1572872 | tf_op jit(solution)/shard_map/ppermute | solution.py:152
  64.3 3.4 collective-permute-start.14
  64.3 5.7 %copy-start.30 = (bf16[4,256,1024]{2,1,0:T(8,128)(2,1)}, bf16[4,256,1024]{2,1,0:T(8,128)(2,1)S(1)}, u32[]{:S(2)}) copy-start(bf16[4,256,1024]{2,1,0:T(8,128)(2,1)S(1)} %bitcast_dynamic-update-slice_fusion.4) | copy-start | bytes 6291460
  64.4 32.3 %collective-permute-start.5 = (bf16[256,1024]{1,0:T(8,128)(2,1)}, bf16[256,1024]{1,0:T(8,128)(2,1)}, u32[]{:S(2)}, u32[]{:S(2)}) collective-permute-start(bf16[256,1024]{1,0:T(8,128)(2,1)} %get-tuple-element.34), channel_id=1, source_target_pairs={{0,3},{1,2},{2,1},{3,0},{4,7},{5,6},{6,5},{7,4},{8,11},{9,10},{10,... | collective-permute-start | bytes 1572872 | tf_op jit(solution)/shard_map/ppermute | solution.py:152
  67.5 31.4 %collective-permute-start.2 = (bf16[144,1024]{1,0:T(8,128)(2,1)}, bf16[144,1024]{1,0:T(8,128)(2,1)}, u32[]{:S(2)}, u32[]{:S(2)}) collective-permute-start(bf16[144,1024]{1,0:T(8,128)(2,1)} %collective-permute-done.1), channel_id=1, source_target_pairs={{0,1},{1,0},{2,3},{3,2},{4,5},{5,4},{6,7},{7,6},{8,9},{9,8},{10,11... | collective-permute-start | bytes 884744 | tf_op jit(solution)/shard_map/ppermute | solution.py:152
  67.7 19.9 %copy-start.43 = (bf16[128,1024]{1,0:T(8,128)(2,1)}, bf16[128,1024]{1,0:T(8,128)(2,1)S(1)}, u32[]{:S(2)}) copy-start(bf16[128,1024]{1,0:T(8,128)(2,1)S(1)} %collective-permute-done.14) | copy-start | bytes 786436
  90.7 10.7 %copy-start.2 = (bf16[1,1,128,1024]{3,2,1,0:T(8,128)(2,1)S(1)}, bf16[1,1,128,1024]{3,2,1,0:T(8,128)(2,1)}, u32[]{:S(2)}) copy-start(bf16[1,1,128,1024]{3,2,1,0:T(8,128)(2,1)} %param.15) | copy-start | bytes 786436
  100.3 4.3 copy-start.51
  101.4 3.2 copy-start.15
  102.1 129.7 %copy-start.52 = (f32[512]{0:T(512)}, f32[512]{0:T(512)S(1)}, u32[]{:S(2)}) copy-start(f32[512]{0:T(512)S(1)} %add_rsqrt_fusion) | copy-start | bytes 6148
  107.7 3.6 copy-start.41
  107.7 3.9 copy-start.39
  115.2 32.2 %all-to-all-start = ((bf16[32,192,128]{2,1,0:T(8,128)(2,1)}), bf16[32,192,128]{2,1,0:T(8,128)(2,1)S(1)}, u32[]{:S(2)}, u32[]{:S(2)}) async-start(bf16[32,192,128]{2,1,0:T(8,128)(2,1)} %pad_maximum_fusion.1), calls=%async_computation | async-start | bytes 3145728 | tf_op jit(solution)/shard_map/all_to_all | solution.py:254
  183.6 27.6 %all-to-all-start.1 = ((bf16[32,192,128]{2,1,0:T(8,128)(2,1)}), bf16[32,192,128]{2,1,0:T(8,128)(2,1)S(1)}, u32[]{:S(2)}, u32[]{:S(2)}) async-start(bf16[32,192,128]{2,1,0:T(8,128)(2,1)} %shard_map.254), calls=%async_computation.1 | async-start | bytes 3145728 | tf_op jit(solution)/shard_map/all_to_all | solution.py:258
  196.6 4.3 copy-start.62
  200.9 4.3 copy-start.12
  200.9 4.3 copy-start.16
  221.7 4.1 copy-start.5
  221.7 4.1 copy-start.7
  225.8 4.8 copy-start.38
  228.1 2.7 copy-start.29
  228.1 3.7 copy-start.10
  228.1 3.6 copy-start.14
  228.2 3.6 copy-start.18
  231.8 6.2 %copy-start.34 = (bf16[1024,768]{1,0:T(8,128)(2,1)S(1)}, bf16[1024,768]{1,0:T(8,128)(2,1)}, u32[]{:S(2)}) copy-start(bf16[1024,768]{1,0:T(8,128)(2,1)} %convolution_convert_fusion.2) | copy-start | bytes 4718596
  238.0 8.0 %copy-start.33 = (bf16[1024,1024]{1,0:T(8,128)(2,1)S(1)}, bf16[1024,1024]{1,0:T(8,128)(2,1)}, u32[]{:S(2)}) copy-start(bf16[1024,1024]{1,0:T(8,128)(2,1)} %convolution_convert_fusion.1) | copy-start | bytes 6291460
  338.0 10.3 %all-to-all-start.3 = ((bf16[4,8,3200]{2,1,0:T(8,128)(2,1)}), bf16[4,8,3200]{2,1,0:T(8,128)(2,1)S(1)}, u32[]{:S(2)}, u32[]{:S(2)}) async-start(bf16[4,8,3200]{2,1,0:T(8,128)(2,1)} %reduce_sum.164), calls=%async_computation.3 | async-start | bytes 409600 | tf_op jit(solution)/shard_map/all_to_all | solution.py:340
  352.0 6.8 %copy-start.59 = (f32[512]{0:T(512)S(1)}, f32[512]{0:T(512)}, u32[]{:S(2)}) copy-start(f32[512]{0:T(512)} %get-tuple-element.61) | copy-start | bytes 6148
  352.0 6.9 %copy-start.58 = (f32[512]{0:T(512)S(1)}, f32[512]{0:T(512)}, u32[]{:S(2)}) copy-start(f32[512]{0:T(512)} %get-tuple-element.60) | copy-start | bytes 6148
  352.0 6.9 %copy-start.57 = (f32[512]{0:T(512)S(1)}, f32[512]{0:T(512)}, u32[]{:S(2)}) copy-start(f32[512]{0:T(512)} %get-tuple-element.15) | copy-start | bytes 6148
  352.0 6.9 %copy-start.56 = (f32[512]{0:T(512)S(1)}, f32[512]{0:T(512)}, u32[]{:S(2)}) copy-start(f32[512]{0:T(512)} %get-tuple-element.19) | copy-start | bytes 6148
  352.0 7.4 %copy-start.61 = (bf16[512,1024]{1,0:T(8,128)(2,1)S(1)}, bf16[512,1024]{1,0:T(8,128)(2,1)}, u32[]{:S(2)}) copy-start(bf16[512,1024]{1,0:T(8,128)(2,1)} %get-tuple-element.22) | copy-start | bytes 3145732
  352.0 127.1 %all-to-all-start.4 = ((bf16[32,8,12544]{2,1,0:T(8,128)(2,1)}), bf16[32,8,12544]{2,1,0:T(8,128)(2,1)}, u32[]{:S(2)}, u32[]{:S(2)}) async-start(bf16[32,8,12544]{2,1,0:T(8,128)(2,1)} %broadcast_in_dim.132), calls=%async_computation.4 | async-start | bytes 12845056 | tf_op jit(solution)/shard_map/all_to_all | solution.py:353
  361.7 2.7 copy-start.1
  365.8 98.2 %collective-permute-start.17 = (bf16[128,2048]{1,0:T(8,128)(2,1)}, bf16[128,2048]{1,0:T(8,128)(2,1)}, u32[]{:S(2)}, u32[]{:S(2)}) collective-permute-start(bf16[128,2048]{1,0:T(8,128)(2,1)} %get-tuple-element.29), channel_id=1, source_target_pairs={{0,3},{1,2},{2,1},{3,0},{4,7},{5,6},{6,5},{7,4},{8,11},{9,10},{10,... | collective-permute-start | bytes 1572872 | tf_op jit(solution)/shard_map/ppermute | solution.py:152
  365.8 110.5 %collective-permute-start.16 = (bf16[128,2048]{1,0:T(8,128)(2,1)}, bf16[128,2048]{1,0:T(8,128)(2,1)}, u32[]{:S(2)}, u32[]{:S(2)}) collective-permute-start(bf16[128,2048]{1,0:T(8,128)(2,1)} %get-tuple-element.30), channel_id=1, source_target_pairs={{0,2},{1,3},{2,0},{3,1},{4,6},{5,7},{6,4},{7,5},{8,10},{9,11},{10,... | collective-permute-start | bytes 1572872 | tf_op jit(solution)/shard_map/ppermute | solution.py:152
  368.3 108.0 %collective-permute-start.15 = (bf16[128,2048]{1,0:T(8,128)(2,1)S(1)}, bf16[128,2048]{1,0:T(8,128)(2,1)}, u32[]{:S(2)}, u32[]{:S(2)}) collective-permute-start(bf16[128,2048]{1,0:T(8,128)(2,1)S(1)} %get-tuple-element.28), channel_id=1, source_target_pairs={{0,1},{1,0},{2,3},{3,2},{4,5},{5,4},{6,7},{7,6},{8,9},{9,8},{10,11... | collective-permute-start | bytes 1572872 | tf_op jit(solution)/shard_map/ppermute | solution.py:152
  369.9 108.2 %copy-start.21 = (bf16[1,1,128,1024]{3,2,1,0:T(8,128)(2,1)S(1)}, bf16[1,1,128,1024]{3,2,1,0:T(8,128)(2,1)}, u32[]{:S(2)}) copy-start(bf16[1,1,128,1024]{3,2,1,0:T(8,128)(2,1)} %param.29) | copy-start | bytes 786436
  492.8 4.9 copy-start.54
  (21 other events, 36.5 us)
